TPU v7x, 256 devices: a whole 4x4x8 slice. The times are simulated.
256 devices in a mesh: tile: 64 (over y_hi, x, z), head: 4 (over y_lo, core).
Axes of the slice: x: 4, y: 4 (y_hi: 2, y_lo: 2; y = y_hi * 2 + y_lo), z: 8, core: 2. Of those that a mesh axis runs over, the one named last changes fastest.
Arguments:
- tokens: bfloat16 [4, 96, 768, 512], P(None, 'head', 'tile'), may hold values from -6 to 6
- land_sea: int32 [96, 768], P('head', 'tile'), may hold values 0 or 1
- land_embed: float32 [2, 512], replicated, may hold values from -6 to 6
- gain_attn: float32 [512], replicated, may hold values from 0.1 to 1.9
- qkv_weight: bfloat16 [3, 512, 512], P(None, None, 'head'), may hold values from -0.25 to 0.25
- out_weight: bfloat16 [512, 512], P('head'), may hold values from -0.25 to 0.25
- bias_left: bfloat16 [8, 144, 32], P('head'), may hold values from -10 to 10
- bias_right: bfloat16 [8, 144, 32], P('head'), may hold values from -10 to 10
- gain_mlp: float32 [512], replicated, may hold values from 0.1 to 1.9
- up_weight: bfloat16 [512, 2048], replicated, may hold values from -0.25 to 0.25
- down_weight: bfloat16 [2048, 512], replicated, may hold values from -0.125 to 0.125
Outputs:
- block_out: bfloat16 [4, 96, 768, 512], P(None, 'head', 'tile')
All inputs are finite; a program needn't handle non-finite values. No bound on the sum of `land_sea` on one device may be relied on, other than what follows from the above.
Results may differ from a plain program's by a relative error of at most 0.011.
Values may be sent and summed in bfloat16 or wider, within the bound.
No kernel may reach another device: no remote copies, remote signals or barrier semaphores. Data moves between devices by JAX's collectives and lax.ppermute only.
A program may use at most 128 MiB of HBM per device.

v0:
```python
import functools

import jax
import jax.numpy as jnp
import numpy as np
from jax import lax
from jax.experimental import pallas as pl
from jax.experimental.pallas import tpu as pltpu
from jax.sharding import PartitionSpec as P

D = 512
AXES = ("tile", "head")
BF = jnp.bfloat16
F32 = jnp.float32
MIB = 2**20
PLACE = {1: (0, 0), 2: (0, 1), 3: (1, 0), 0: (1, 1)}
NT = (((1,), (1,)), ((), ()))
PENALTY = -1000000000.0
VMEM = pl.BlockSpec(memory_space=pltpu.VMEM)
SMEM = pl.BlockSpec(memory_space=pltpu.SMEM)
ANY = pl.BlockSpec(memory_space=pl.ANY)
HBM = pl.BlockSpec(memory_space=pltpu.HBM)


def dot(left, right):
    return jnp.dot(left, right, preferred_element_type=F32)


def dot_nt(left, right):
    return lax.dot_general(left, right, NT, preferred_element_type=F32)


def layer_norm(values, norm_gain):
    average = jnp.mean(values, axis=-1, keepdims=True)
    centred = values - average
    variance = jnp.mean(centred * centred, axis=-1, keepdims=True)
    return centred * lax.rsqrt(variance + 1e-05) * norm_gain


class Copies:
    def __init__(self, sems):
        self.sems, self.count = sems, 0

    def __call__(self, source, target):
        one = pltpu.make_async_copy(source, target, self.sems.at[self.count])
        one.start()
        self.count += 1
        return one


def wait_all(copies):
    for one in copies:
        one.wait()


def pack_kernel(wqkv, wo, left, right, out, whole, factors, sems):
    copy = Copies(sems)
    small = [copy(left, factors.at[0]), copy(right, factors.at[1])]
    loads = [copy(wqkv, whole.at[:1536])]
    for block in range(4):
        lanes = pl.ds(128 * block, 128)
        loads.append(copy(wo.at[:, lanes], whole.at[pl.ds(1536 + 128 * block, 128)]))
    wait_all(small)
    for index in range(2):
        base = 2048 + 128 * index
        whole[base : base + 64, :] = factors[index, :, :128]
        whole[base + 64 : base + 128, :] = jnp.concatenate(
            (factors[index, :, 128:], jnp.zeros((64, 112), BF)), axis=1
        )
    wait_all(loads)
    wait_all([copy(whole, out)])


def norm_kernel(
    tokens_in, land_in, embed_in, gain_in, gain_mlp_in, after,
    norm_b_out, norm_a_out, resid_b_out, resid_a_out, gain_mlp_out,
    tokens, land, embed, gain, gain_mlp, norm, resid, sems,
):
    parity = lax.rem(lax.axis_index("tile"), 2)
    copy = Copies(sems)
    small = [copy(land_in, land), copy(embed_in, embed), copy(gain_in, gain), copy(gain_mlp_in, gain_mlp)]
    loads = [copy(tokens_in.at[:, 1 - parity], tokens.at[1]), copy(tokens_in.at[:, parity], tokens.at[0])]
    wait_all(small)
    stores = [copy(gain_mlp, gain_mlp_out)]
    eye = lax.broadcasted_iota(jnp.int32, (24, 24), 0) == lax.broadcasted_iota(jnp.int32, (24, 24), 1)
    columns = dot_nt(eye.astype(F32), land[...].astype(F32))
    sea_row, land_row = embed[0:1, :], embed[1:2, :]
    for half in (1, 0):
        side = parity if half == 0 else 1 - parity
        mine = jnp.where(side == 0, columns[:, :6], columns[:, 6:])
        loads[1 - half].wait()
        for col in range(6):
            added = jnp.where(mine[:, col : col + 1] > 0.5, land_row, sea_row)
            for level in range(4):
                pair, inner = PLACE[level]
                row = tokens[half, level, col].astype(F32) + added
                for k in range(3):
                    at = (pair * 3 + k) * 72 + inner * 36 + col * 6
                    resid[half, at : at + 6, :] = row[3 + 6 * k : 9 + 6 * k, :]
                at = 432 + pair * 40 + inner * 18 + col * 3
                resid[half, at : at + 3, :] = row[:3, :]
                resid[half, at + 80 : at + 83, :] = row[21:, :]
        for at in (468, 508, 548, 588):
            resid[half, at : at + 4, :] = jnp.zeros((4, D), F32)
        stores.append(copy(resid.at[half], (resid_a_out, resid_b_out)[half]))
        for start, count in ((0, 144), (144, 144), (288, 144), (432, 160)):
            rows = slice(start, start + count)
            norm[half, rows, :] = layer_norm(resid[half, rows, :], gain[...]).astype(BF)
        stores.append(copy(norm.at[half], (norm_a_out, norm_b_out)[half]))
    wait_all(stores)


def block_rows(block):
    return (72 * block, 72) if block < 6 else (432 + 80 * (block - 6), 80)


def repeat4(value):
    return jnp.concatenate((value,) * 4, axis=0)


def head_stack(value, width):
    lane = lax.broadcasted_iota(jnp.int32, value.shape, 1) // width
    return jnp.concatenate(
        [jnp.where(lane == head, value, 0.0) for head in range(4)], axis=0
    ).astype(BF)


def head_pick(stacked):
    count = stacked.shape[0] // 4
    lane = lax.broadcasted_iota(jnp.int32, (count, stacked.shape[1]), 1) // 64
    total = stacked[:count]
    for head in range(1, 4):
        total = jnp.where(lane == head, stacked[count * head : count * head + count], total)
    return total


def qkv_kernel(group, norm_a, norm_b, pos_query, pos_key, *refs):
    parts, norms = refs[:2], (norm_a, norm_b)
    query, key, value, wkv, wo, bias_in, bias_edge = refs[2:9]
    wq, left, right = refs[-3:]
    def part(source, row, count):
        return parts[source][row : row + count, :]

    for source in range(2):
        lanes = slice(128 * source, 128 * source + 128)
        wq[:, lanes] = part(source, 0, 512)
        wkv[:, lanes] = part(source, 512, 512)
        more = slice(256 + 128 * source, 384 + 128 * source)
        wkv[:, more] = part(source, 1024, 512)
        for block in range(4):
            wo[lanes, 128 * block : 128 * block + 128] = part(source, 1536 + 128 * block, 128)
        rows = slice(64 * source, 64 * source + 64)
        left[rows, :128] = part(source, 2048, 64)
        left[rows, 128:] = part(source, 2112, 64)
        right[rows, :128] = part(source, 2176, 64)
        right[rows, 128:] = part(source, 2240, 64)
    factors = dot_nt(pos_query[...], left[...])
    q_level = lax.broadcasted_iota(jnp.int32, (72, 144), 0) >= 36
    k_level = lax.rem(lax.broadcasted_iota(jnp.int32, (72, 144), 1), 72) >= 36
    split = repeat4(jnp.where(q_level == k_level, 0.0, PENALTY))
    row = lax.broadcasted_iota(jnp.int32, (40, 160), 0)
    lane = lax.broadcasted_iota(jnp.int32, (40, 160), 1)
    slot = lax.rem(lane, 40)
    halo = lax.rem(lane // 40, 2) == 1
    head = lax.axis_index("head")
    for half in range(2):
        own_rows = head_stack(factors[72 * half : 72 * half + 72, :], 32)
        keys = dot_nt(right[...], pos_key[144 * half : 144 * half + 144, :]).astype(BF)
        bias = dot(own_rows, keys)
        bias_in[half, 0] = bias
        bias_in[half, 1] = bias + split
        for side in range(2):
            at = 144 + 80 * half + 40 * (1 - side)
            own_rows = head_stack(factors[at : at + 40, :], 32)
            at = 288 + 320 * half + 160 * side
            keys = dot_nt(right[...], pos_key[at : at + 160, :]).astype(BF)
            bias = dot(own_rows, keys)
            outside = jnp.logical_and(halo, head == 3 * side)
            hidden = jnp.logical_or(slot >= 36, outside)
            bias_edge[half, side, 0] = bias + repeat4(jnp.where(hidden, PENALTY, 0.0))
            hidden = jnp.logical_or(hidden, (row >= 18) != (slot >= 18))
            bias_edge[half, side, 1] = bias + repeat4(jnp.where(hidden, PENALTY, 0.0))
    for half, norm in enumerate(norms):
        got_q = dot(norm[...], wq[...]) * 0.125
        got_kv = dot(norm[...], wkv[...])
        for block in range(8):
            at, count = block_rows(block)
            query[half, block, :count] = got_q[at : at + count].astype(BF)
            key[half, block, :count] = got_kv[at : at + count, :256].astype(BF)
            value[half, block, :count] = got_kv[at : at + count, 256:].astype(BF)


def attend(query, keys, values, bias):
    scores = dot_nt(head_stack(query, 64), keys) + bias[...]
    weights = jnp.exp(scores - jnp.max(scores, axis=-1, keepdims=True))
    scale = 1.0 / jnp.sum(weights, axis=-1, keepdims=True)
    return head_pick(dot(weights.astype(BF), values) * scale)


def fetch_kernel(up_in, down_in, after, up, down, sems):
    copies = (
        pltpu.make_async_copy(up_in, up, sems.at[0]),
        pltpu.make_async_copy(down_in, down, sems.at[1]),
    )
    for one in copies:
        one.start()
    for one in copies:
        one.wait()


def feed_forward(heads, resid, wo_0, wo_1, gain, up, down, hidden):
    mixed = resid + dot(heads[0].astype(BF), wo_0[...]) + dot(heads[1].astype(BF), wo_1[...])
    second = layer_norm(mixed, gain[...]).astype(BF)
    for start in range(0, 2048, 512):
        inner = dot(second, up[:, start : start + 512])
        inner = 0.5 * inner * (1.0 + lax.erf(inner * 0.7071067811865476))
        hidden[:, start : start + 512] = inner.astype(BF)
    return mixed + dot(hidden[...], down[...])


def half_kernel(half, remote, resid, gain, up, down, *refs):
    groups = (refs[:6], refs[6:12])
    out, edge_key, edge_value, keys, values, heads, hidden, inside = refs[12:]
    for group, (query, key, value, wkv, wo, bias) in enumerate(groups):
        got = dot(remote[...], wkv[...])
        for lanes, near, target, edge in ((0, key, keys, edge_key), (256, value, values, edge_value)):
            for block in range(8):
                at, count = block_rows(block)
                part = got[at : at + count, lanes : lanes + 256]
                if block < 6:
                    joined = jnp.concatenate((near[half, block, :72].astype(F32), part), axis=0)
                    target[block] = joined.astype(BF)
                else:
                    edge[group, block - 6] = part.astype(BF)
        for block in range(6):
            heads[group, 72 * block : 72 * block + 72, :] = attend(
                query[half, block, :72].astype(F32), keys[block], values[block], bias.at[half, block // 3]
            )
    inside[...] = feed_forward(
        heads, resid[:432, :], groups[0][4], groups[1][4], gain, up, down, hidden
    )
    for level in range(4):
        pair, inner = PLACE[level]
        for col in range(6):
            for k in range(3):
                at = (pair * 3 + k) * 72 + inner * 36 + col * 6
                out[level, col, 3 + 6 * k : 9 + 6 * k, :] = inside[at : at + 6, :]
            out[level, col, :3, :] = jnp.zeros((3, D), F32)
            out[level, col, 21:, :] = jnp.zeros((3, D), F32)


def gather_kernel(count, *refs):
    blocks, (first, second) = refs[:count], refs[-2:]
    odd = lax.rem(lax.axis_index("head"), 2) == 1
    for index, block in enumerate(blocks):
        rows = slice(80 * index, 80 * index + 80)
        top, bottom = block[432:512, :], block[512:592, :]
        first[rows, :] = jnp.where(odd, top, bottom)
        second[rows, :] = jnp.where(odd, bottom, top)


def side_of(which):
    odd = lax.rem(lax.axis_index("head"), 2)
    return odd if which else 1 - odd


def edge_attend(which, exchange, remotes, groups, halo, heads):
    side = side_of(which)
    for group, (query, key, value, wkv, wo, bias) in enumerate(groups):
        halo[...] = dot(exchange[...], wkv[...])
        for half in range(2):
            near, far = ((160, 240), (0, 80))[half]
            own_query = query[half, 6 + side].astype(F32)
            own = [ref[half, 6 + side].astype(F32) for ref in (key, value)]
            other = [ref[group, side].astype(F32) for ref in remotes[half]]
            for pair in range(2):
                rows = slice(40 * pair, 40 * pair + 40)
                joined = []
                for index in range(2):
                    lanes = slice(256 * index, 256 * index + 256)
                    parts = (
                        own[index][rows], halo[near + 40 * pair : near + 40 * pair + 40, lanes],
                        other[index][rows], halo[far + 40 * pair : far + 40 * pair + 40, lanes],
                    )
                    joined.append(jnp.concatenate(parts, axis=0).astype(BF))
                got = attend(own_query[rows], joined[0], joined[1], bias.at[half, side, pair])
                at = 144 * which + 72 * half + 36 * pair
                heads[group, at : at + 36, :] = got[:36]


def first_edge_kernel(first, key_a, value_a, key_b, value_b, *refs):
    groups, (heads, halo) = (refs[:6], refs[6:12]), refs[12:]
    edge_attend(0, first, ((key_a, value_a), (key_b, value_b)), groups, halo, heads)


def edge_kernel(
    second, key_a, value_a, key_b, value_b, before, resid_a, resid_b, gain, out_a, out_b, up, down, *refs
):
    groups = (refs[:6], refs[6:12])
    out, halo, heads, resid, edges, stage, hidden, sems = refs[12:]
    parity = lax.rem(lax.axis_index("tile"), 2)
    heads[:, :144, :] = before[...]
    edge_attend(1, second, ((key_a, value_a), (key_b, value_b)), groups, halo, heads)
    for which in range(2):
        for half, source in enumerate((resid_a, resid_b)):
            for pair in range(2):
                start = pl.multiple_of(432 + 80 * side_of(which) + 40 * pair, 8)
                at = 144 * which + 72 * half + 36 * pair
                resid[at : at + 36, :] = source[pl.ds(start, 40), :][:36]
    done = feed_forward(heads, resid[...], groups[0][4], groups[1][4], gain, up, down, hidden)
    edges[0] = done[:144]
    edges[1] = done[144:]
    odd = lax.rem(lax.axis_index("head"), 2)
    copies = []
    for half, inside in enumerate((out_a, out_b)):
        place = parity if half == 0 else 1 - parity
        for level in range(4):
            pair, inner = PLACE[level]
            for col in range(6):
                at = 72 * half + pair * 36 + inner * 18 + col * 3
                whole = (
                    edges[1 - odd, at : at + 3, :], inside[level, col, 3:21, :], edges[odd, at : at + 3, :]
                )
                stage[half, level, col] = jnp.concatenate(whole, axis=0).astype(BF)
            copies.append(
                pltpu.make_async_copy(stage.at[half, level], out.at[level, place], sems.at[4 * half + level])
            )
            copies[-1].start()
    wait_all(copies)


def call(kernel, out_shape, in_specs, scratch=(), limit=16, flops=0, out_specs=None, **extra):
    many = isinstance(out_shape, (list, tuple))
    return pl.pallas_call(
        kernel,
        out_shape=out_shape,
        in_specs=in_specs,
        out_specs=out_specs or ([VMEM] * len(out_shape) if many else VMEM),
        scratch_shapes=scratch,
        compiler_params=pltpu.CompilerParams(vmem_limit_bytes=limit * MIB),
        cost_estimate=pl.CostEstimate(flops=flops, bytes_accessed=2 * MIB, transcendentals=0),
        **extra,
    )


def shape(*dims, dtype=BF):
    return jax.ShapeDtypeStruct(dims, dtype)


def position_tables():
    tables = []
    for parity in range(2):
        columns = (1 - parity, parity)

        def inside(half):
            c = columns[half]
            return [l * 72 + r * 12 + 6 * c + col for l in range(2) for col in range(6) for r in range(6)]

        def edge(half, rows):
            c = columns[half]
            spots = [
                l * 72 + (3 * rows + r) * 12 + 6 * c + col
                for l in range(2) for col in range(6) for r in range(3)
            ]
            return spots + [-1] * 4

        query = inside(0) + inside(1)
        for half in range(2):
            query += edge(half, 0) + edge(half, 1)
        key = []
        for half in range(2):
            key += inside(half) + inside(1 - half)
        for half in range(2):
            for side in range(2):
                near = 1 - side
                for h in (half, 1 - half):
                    key += edge(h, near) + edge(h, 1 - near)
        tables.append(query + key)
    return np.array(tables, np.int32)


def pairs_of(tiles, move):
    pairs = []
    for tile in range(tiles):
        for head in range(4):
            target = move(tile, head)
            if target is not None:
                pairs.append((tile * 4 + head, (target[0] % tiles) * 4 + target[1]))
    return pairs


def shards(
    tokens, land_sea, land_embed, gain_attn, qkv_weight, out_weight, bias_left, bias_right,
    gain_mlp, up_weight, down_weight,
):
    tiles = lax.axis_size("tile")
    parity = lax.rem(lax.axis_index("tile"), 2)

    def along_y(t, h):
        high, rest = divmod(t, tiles // 2)
        y = (2 * high + h // 2 + (-1 if h % 2 else 1)) % 4
        return (y // 2) * (tiles // 2) + rest, (y % 2) * 2 + h % 2

    def send(value, move):
        return lax.ppermute(value, AXES, pairs_of(tiles, move))

    swap_a = lambda t, h: (t + 1 if t % 2 else t - 1, h)
    swap_b = lambda t, h: (t ^ 1, h)
    swap_core = lambda t, h: (t, h ^ 1)
    swap_chip = lambda t, h: (t, 3 - h) if h in (1, 2) else None

    pack = call(
        pack_kernel,
        shape(2304, 128),
        [HBM] * 4,
        [pltpu.VMEM((2304, 128), BF), pltpu.VMEM((2, 64, 144), BF), pltpu.SemaphoreType.DMA((8,))],
        limit=63,
        out_specs=HBM,
        name="pack",
    )(
        qkv_weight.reshape(1536, 128),
        out_weight,
        bias_left.transpose(0, 2, 1).reshape(64, 144),
        bias_right.transpose(0, 2, 1).reshape(64, 144),
    )
    far = send(pack, along_y)

    grid = tokens.transpose(0, 2, 1, 3).reshape(4, 2, 6, 24, D)
    rows = [shape(592, D)] * 2 + [shape(592, D, dtype=F32)] * 2
    norm_b, norm_a, resid_b, resid_a, gain_mlp = call(
        norm_kernel,
        rows + [shape(1, D, dtype=F32)],
        [HBM] * 6,
        [
            pltpu.VMEM((2, 4, 6, 24, D), BF), pltpu.VMEM((12, 24), jnp.int32), pltpu.VMEM((2, D), F32),
            pltpu.VMEM((1, D), F32), pltpu.VMEM((1, D), F32), pltpu.VMEM((2, 592, D), BF),
            pltpu.VMEM((2, 592, D), F32), pltpu.SemaphoreType.DMA((11,)),
        ],
        limit=63,
        out_specs=[HBM] * 5,
        name="norm",
    )(grid, land_sea.transpose(1, 0), land_embed, gain_attn[None], gain_mlp[None], pack)

    remote_b = send(norm_b, swap_b)
    remote_a = send(norm_a, swap_a)
    own, far = lax.optimization_barrier((pack, far))
    mate = send(own, swap_core)
    forwarded = send(far, swap_core)

    places = jnp.asarray(position_tables())
    places = jnp.where(parity == 1, places[1], places[0])
    onehot = (places[:, None] == jnp.arange(256, dtype=jnp.int32)[None, :]).astype(BF)
    def run_qkv(group, norms, parts):
        return call(
            functools.partial(qkv_kernel, group),
            [shape(2, 8, 80, 256)] * 3
            + [shape(D, 512), shape(256, D)]
            + [shape(2, 2, 288, 144, dtype=F32), shape(2, 2, 2, 160, 160, dtype=F32)],
            [VMEM] * 6,
            [pltpu.VMEM((D, 256), BF)] + [pltpu.VMEM((128, 256), BF)] * 2,
            flops=2 * 10**9,
            name="qkv_" + str(group),
        )(*norms, onehot[:304], onehot[304:], *parts)

    near = run_qkv(0, (norm_a, norm_b), (own, far))
    up, down = call(
        fetch_kernel, [shape(D, 2048), shape(2048, D)], [HBM] * 3,
        [pltpu.SemaphoreType.DMA((2,))], flops=10**9, name="fetch",
    )(up_weight, down_weight, near[3])
    rest = run_qkv(1, (norm_a, norm_b), (mate, forwarded))
    heads = near[:6] + rest[:6]

    def run_half(half, remote, resid):
        return call(
            functools.partial(half_kernel, half),
            [shape(4, 6, 24, D, dtype=F32), shape(2, 2, 80, 256), shape(2, 2, 80, 256)],
            [VMEM] * 17,
            [
                pltpu.VMEM((6, 144, 256), BF), pltpu.VMEM((6, 144, 256), BF),
                pltpu.VMEM((2, 432, 256), F32), pltpu.VMEM((432, 2048), BF),
                pltpu.VMEM((432, D), F32),
            ],
            flops=4 * 10**9,
            name="half_" + "ab"[half],
        )(remote, resid, gain_mlp, up, down, *heads)

    inner_b, key_b, value_b = run_half(1, remote_b, resid_b)
    def run_gather(blocks, after, name):
        first, second = call(
            functools.partial(gather_kernel, len(blocks)),
            [shape(80 * len(blocks), D)] * 2, [VMEM] * len(blocks) + [ANY], name=name,
        )(*blocks, after)
        return send(first, swap_core), send(second, swap_chip)

    first, second = run_gather((norm_b, remote_b, norm_a, remote_a), key_b, "gather")
    inner_a, key_a, value_a = run_half(0, remote_a, resid_a)

    remotes = (key_a, value_a, key_b, value_b)
    edge_heads = (*near[:5], near[6], *rest[:5], rest[6])
    before = call(
        first_edge_kernel,
        shape(2, 144, 256, dtype=F32),
        [VMEM] * 17,
        [pltpu.VMEM((320, 512), F32)],
        flops=10**9,
        name="edge_first",
    )(first, *remotes, *edge_heads)
    out = call(
        edge_kernel,
        shape(4, 2, 6, 24, D),
        [VMEM] * 25,
        [
            pltpu.VMEM((320, 512), F32), pltpu.VMEM((2, 288, 256), F32), pltpu.VMEM((288, D), F32),
            pltpu.VMEM((2, 144, D), F32), pltpu.VMEM((2, 4, 6, 24, D), BF), pltpu.VMEM((288, 2048), BF),
            pltpu.SemaphoreType.DMA((8,)),
        ],
        out_specs=ANY,
        flops=4 * 10**9,
        name="edge",
    )(second, *remotes, before, resid_a, resid_b, gain_mlp, inner_a, inner_b, up, down, *edge_heads)
    return out.reshape(4, 12, 24, D).transpose(0, 2, 1, 3)


def solution(mesh):
    in_specs = (
        P(None, "head", "tile", None),
        P("head", "tile"),
        P(),
        P(),
        P(None, None, "head"),
        P("head", None),
        P("head", None, None),
        P("head", None, None),
        P(),
        P(),
        P(),
    )
    out_specs = P(None, "head", "tile", None)
    return jax.shard_map(shards, mesh=mesh, in_specs=in_specs, out_specs=out_specs, check_vma=False)
```

profile of v0, /device:TPU:1, one launch (start us, length us, event | category | flops | bytes accessed | tf_op | source)
XLA Modules:
  0.0 46.1 jit_solution(1823604099604504882)
XLA Ops:
  0.0 0.0 copy-start.8
  0.0 0.0 copy-start.9
  0.0 2.0 %pack.1.after.refs_0_ = bf16[2304,128]{1,0:T(8,128)(2,1)} custom-call(bf16[1536,128]{1,0:T(8,128)(2,1)} %bitcast.17, bf16[128,512]{1,0:T(8,128)(2,1)} %wo.1, bf16[64,144]{1,0:T(8,128)(2,1)} %bitcast.18, bf16[64,144]{1,0:T(8,128)(2,1)} %bitcast.19), custom_call_target="tpu_custom_call" | custom-call | bytes 2097152 | tf_op jit(solution)/shard_map/pack/pallas_call | solution.py:412
  2.0 0.0 copy-start
  2.0 3.6 %collective-permute-start.2 = (bf16[2304,128]{1,0:T(8,128)(2,1)}, bf16[2304,128]{1,0:T(8,128)(2,1)}, u32[]{:S(2)}, u32[]{:S(2)}) collective-permute-start(bf16[2304,128]{1,0:T(8,128)(2,1)} %pack.1.after.refs_0_), channel_id=1, source_target_pairs={{0,2},{1,131},{2,128},{3,1},{4,6},{5,135},{6,132},{7,5},{8,10},{9,... | collective-permute-start | bytes 1769480 | tf_op jit(solution)/shard_map/ppermute | solution.py:405
  5.6 3.4 %norm.1 = (bf16[592,512]{1,0:T(8,128)(2,1)}, bf16[592,512]{1,0:T(8,128)(2,1)}, f32[592,512]{1,0:T(8,128)}, f32[592,512]{1,0:T(8,128)}, f32[1,512]{1,0:T(1,128)}) custom-call(bf16[4,2,6,24,512]{4,3,2,1,0:T(8,128)(2,1)} %bitcast.16, s32[12,24]{1,0:T(8,128)} %bitcast.20, f32[2,512]{1,0:T(2,128)} %embed_in.1, f32[1,512]{1,0:T(1,128)} %bitcast.21, ...), custom_call_target="tpu_custom_call" | custom-call | bytes 2097152 | tf_op jit(solution)/shard_map/norm/pallas_call | solution.py:430
  9.0 0.0 copy-start.5
  9.0 0.0 copy-start.6
  9.0 1.7 %collective-permute-start = (bf16[592,512]{1,0:T(8,128)(2,1)}, bf16[592,512]{1,0:T(8,128)(2,1)S(1)}, u32[]{:S(2)}, u32[]{:S(2)}) collective-permute-start(bf16[592,512]{1,0:T(8,128)(2,1)} %get-tuple-element.36.norm_b.refs_0_), channel_id=1, source_target_pairs={{0,4},{1,5},{2,6},{3,7},{4,0},{5,1},{6,2},{7,3},{8,12},{9,13},{10,... | collective-permute-start | bytes 1818632 | tf_op jit(solution)/shard_map/ppermute | solution.py:405
  10.7 6.9 %collective-permute-start.1 = (bf16[592,512]{1,0:T(8,128)(2,1)}, bf16[592,512]{1,0:T(8,128)(2,1)S(1)}, u32[]{:S(2)}, u32[]{:S(2)}) collective-permute-start(bf16[592,512]{1,0:T(8,128)(2,1)} %get-tuple-element.37.norm_a.refs_2_), channel_id=1, source_target_pairs={{0,252},{1,253},{2,254},{3,255},{4,8},{5,9},{6,10},{7,11},{8,4},{9... | collective-permute-start | bytes 1818632 | tf_op jit(solution)/shard_map/ppermute | solution.py:405
  17.7 0.0 copy-done.8
  17.7 0.0 copy-done.9
  17.7 0.0 collective-permute-done.2.refs_1_
  17.7 0.0 copy-done
  17.7 2.4 %collective-permute-start.3 = (bf16[2304,128]{1,0:T(8,128)(2,1)S(1)}, bf16[2304,128]{1,0:T(8,128)(2,1)S(1)}, u32[]{:S(2)}, u32[]{:S(2)}) collective-permute-start(bf16[2304,128]{1,0:T(8,128)(2,1)S(1)} %copy-done), channel_id=1, source_target_pairs={{0,1},{1,0},{2,3},{3,2},{4,5},{5,4},{6,7},{7,6},{8,9},{9,8},{10,11... | collective-permute-start | bytes 1769480 | tf_op jit(solution)/shard_map/ppermute | solution.py:405
  20.1 0.3 collective-permute-start.4
  20.4 0.2 fusion
  20.7 0.0 copy-done.5
  20.7 0.0 copy-done.6
  20.7 0.0 copy-start.1
  20.8 0.0 copy-start.2
  20.8 3.1 %qkv_0.1 = (bf16[2,8,80,256]{3,2,1,0:T(8,128)(2,1)S(1)}, bf16[2,8,80,256]{3,2,1,0:T(8,128)(2,1)S(1)}, bf16[2,8,80,256]{3,2,1,0:T(8,128)(2,1)S(1)}, bf16[512,512]...) custom-call(bf16[592,512]{1,0:T(8,128)(2,1)S(1)} %copy-done.6, ...), custom_call_target="tpu_custom_call" | custom-call | flops 2000000000 | bytes 2097152 | tf_op jit(solution)/shard_map/qkv_0/pallas_call | solution.py:454
  23.9 0.0 copy-done.1
  23.9 0.0 copy-done.2
  23.9 0.3 fetch.1
  24.2 0.0 copy-start.3
  24.3 0.0 copy-start.7
  24.3 0.0 collective-permute-done.3.refs_0_
  24.3 0.0 collective-permute-done.4.refs_1_
  24.3 1.9 %qkv_1.1 = (bf16[2,8,80,256]{3,2,1,0:T(8,128)(2,1)S(1)}, bf16[2,8,80,256]{3,2,1,0:T(8,128)(2,1)S(1)}, bf16[2,8,80,256]{3,2,1,0:T(8,128)(2,1)S(1)}, bf16[512,512]...) custom-call(bf16[592,512]{1,0:T(8,128)(2,1)S(1)} %copy-done.6, ...), custom_call_target="tpu_custom_call" | custom-call | flops 2000000000 | bytes 2097152 | tf_op jit(solution)/shard_map/qkv_1/pallas_call | solution.py:454
  26.2 0.0 collective-permute-done.remote.refs_1_
  26.2 0.0 copy-done.3
  26.2 0.0 copy-done.7
  26.2 4.8 %half_b.1 = (f32[4,6,24,512]{3,2,1,0:T(8,128)S(1)}, bf16[2,2,80,256]{3,2,1,0:T(8,128)(2,1)S(1)}, bf16[2,2,80,256]{3,2,1,0:T(8,128)(2,1)S(1)}) custom-call(bf16[592,512]{1,0:T(8,128)(2,1)S(1)} %collective-permute-done.remote.refs_1_, f32[592,512]{1,0:T(8,128)S(1)} %copy-done.3, f32[1,512]{1,0:T(1,128)S(1)} %copy-done.7, ...), custom_call_target="tpu_custom_call" | custom-call | flops 4000000000 | bytes 2097152 | tf_op jit(solution)/shard_map/half_b/pallas_call | solution.py:474
  31.0 0.0 collective-permute-done.1.refs_3_.remote
  31.0 0.0 copy-start.4
  31.0 0.1 gather.1
  31.1 4.1 %collective-permute-start.5 = (bf16[320,512]{1,0:T(8,128)(2,1)S(1)}, bf16[320,512]{1,0:T(8,128)(2,1)S(1)}, u32[]{:S(2)}, u32[]{:S(2)}) collective-permute-start(bf16[320,512]{1,0:T(8,128)(2,1)S(1)} %get-tuple-element.57), channel_id=1, source_target_pairs={{1,2},{2,1},{5,6},{6,5},{9,10},{10,9},{13,14},{14,13},{17,18},{18,... | collective-permute-start | bytes 983048 | tf_op jit(solution)/shard_map/ppermute | solution.py:405
  35.2 0.3 collective-permute-start.6
  35.5 0.0 copy-done.4
  35.5 4.8 %half_a.1 = (f32[4,6,24,512]{3,2,1,0:T(8,128)S(1)}, bf16[2,2,80,256]{3,2,1,0:T(8,128)(2,1)S(1)}, bf16[2,2,80,256]{3,2,1,0:T(8,128)(2,1)S(1)}) custom-call(bf16[592,512]{1,0:T(8,128)(2,1)S(1)} %collective-permute-done.1.refs_3_.remote, f32[592,512]{1,0:T(8,128)S(1)} %copy-done.4, f32[1,512]{1,0:T(1,128)S(1)} %copy-done.7, ...), custom_call_target="tpu_custom_call" | custom-call | flops 4000000000 | bytes 2097152 | tf_op jit(solution)/shard_map/half_a/pallas_call | solution.py:474
  40.3 0.0 collective-permute-done.6.first
  40.3 1.3 %edge_first.1.before = f32[2,144,256]{2,1,0:T(8,128)S(1)} custom-call(bf16[320,512]{1,0:T(8,128)(2,1)S(1)} %collective-permute-done.6.first, bf16[2,2,80,256]{3,2,1,0:T(8,128)(2,1)S(1)} %get-tuple-element.59.key_a, bf16[2,2,80,256]{3,2,1,0:T(8,128)(2,1)S(1)} %get-tuple-element.60.value_a, bf16[2,2,80,256]{3,2,1,0:T(8,128)(2,1)S(1)} %get-tuple-element.56.refs_4_.key_b, ...), custom_call_target="tpu_custom_call" | custom-call | flops 1000000000 | bytes 2097152 | tf_op jit(solution)/shard_map/edge_first/pallas_call | solution.py:500
  41.6 0.0 collective-permute-done.5.second
  41.6 4.3 %edge.1 = bf16[4,2,6,24,512]{4,3,2,1,0:T(8,128)(2,1)} custom-call(bf16[320,512]{1,0:T(8,128)(2,1)S(1)} %collective-permute-done.5.second, bf16[2,2,80,256]{3,2,1,0:T(8,128)(2,1)S(1)} %get-tuple-element.59.key_a, bf16[2,2,80,256]{3,2,1,0:T(8,128)(2,1)S(1)} %get-tuple-element.60.value_a, bf16[2,2,80,256]{3,2,1,0:T(8,128)(2,1)S(1)} %get-tuple-element.56.refs_4_.key_b, ...), custom_call_target="tpu_custom_call" | custom-call | flops 4000000000 | bytes 2097152 | tf_op jit(solution)/shard_map/edge/pallas_call | solution.py:508
  (3 shorter events, 0.1 us)
Async XLA Ops:
  0.0 17.7 %copy-start.8 = (s32[1,1232]{1,0:T(1,128)S(1)}, s32[1,1232]{1,0:T(1,128)}, u32[]{:S(2)}) copy-start(s32[1,1232]{1,0:T(1,128)} %constant.19) | copy-start | bytes 14788
  0.0 17.7 %copy-start.9 = (s32[1,1232]{1,0:T(1,128)S(1)}, s32[1,1232]{1,0:T(1,128)}, u32[]{:S(2)}) copy-start(s32[1,1232]{1,0:T(1,128)} %constant.20) | copy-start | bytes 14788
  2.0 15.7 %copy-start = (bf16[2304,128]{1,0:T(8,128)(2,1)S(1)}, bf16[2304,128]{1,0:T(8,128)(2,1)}, u32[]{:S(2)}) copy-start(bf16[2304,128]{1,0:T(8,128)(2,1)} %pack.1.after.refs_0_) | copy-start | bytes 1769476
  2.0 15.7 %collective-permute-start.2 = (bf16[2304,128]{1,0:T(8,128)(2,1)}, bf16[2304,128]{1,0:T(8,128)(2,1)}, u32[]{:S(2)}, u32[]{:S(2)}) collective-permute-start(bf16[2304,128]{1,0:T(8,128)(2,1)} %pack.1.after.refs_0_), channel_id=1, source_target_pairs={{0,2},{1,131},{2,128},{3,1},{4,6},{5,135},{6,132},{7,5},{8,10},{9,... | collective-permute-start | bytes 1769480 | tf_op jit(solution)/shard_map/ppermute | solution.py:405
  9.0 11.7 %copy-start.5 = (bf16[592,512]{1,0:T(8,128)(2,1)S(1)}, bf16[592,512]{1,0:T(8,128)(2,1)}, u32[]{:S(2)}) copy-start(bf16[592,512]{1,0:T(8,128)(2,1)} %get-tuple-element.36.norm_b.refs_0_) | copy-start | bytes 1818628
  9.0 11.7 %copy-start.6 = (bf16[592,512]{1,0:T(8,128)(2,1)S(1)}, bf16[592,512]{1,0:T(8,128)(2,1)}, u32[]{:S(2)}) copy-start(bf16[592,512]{1,0:T(8,128)(2,1)} %get-tuple-element.37.norm_a.refs_2_) | copy-start | bytes 1818628
  9.0 17.2 %collective-permute-start = (bf16[592,512]{1,0:T(8,128)(2,1)}, bf16[592,512]{1,0:T(8,128)(2,1)S(1)}, u32[]{:S(2)}, u32[]{:S(2)}) collective-permute-start(bf16[592,512]{1,0:T(8,128)(2,1)} %get-tuple-element.36.norm_b.refs_0_), channel_id=1, source_target_pairs={{0,4},{1,5},{2,6},{3,7},{4,0},{5,1},{6,2},{7,3},{8,12},{9,13},{10,... | collective-permute-start | bytes 1818632 | tf_op jit(solution)/shard_map/ppermute | solution.py:405
  10.7 20.3 %collective-permute-start.1 = (bf16[592,512]{1,0:T(8,128)(2,1)}, bf16[592,512]{1,0:T(8,128)(2,1)S(1)}, u32[]{:S(2)}, u32[]{:S(2)}) collective-permute-start(bf16[592,512]{1,0:T(8,128)(2,1)} %get-tuple-element.37.norm_a.refs_2_), channel_id=1, source_target_pairs={{0,252},{1,253},{2,254},{3,255},{4,8},{5,9},{6,10},{7,11},{8,4},{9... | collective-permute-start | bytes 1818632 | tf_op jit(solution)/shard_map/ppermute | solution.py:405
  17.7 6.6 %collective-permute-start.3 = (bf16[2304,128]{1,0:T(8,128)(2,1)S(1)}, bf16[2304,128]{1,0:T(8,128)(2,1)S(1)}, u32[]{:S(2)}, u32[]{:S(2)}) collective-permute-start(bf16[2304,128]{1,0:T(8,128)(2,1)S(1)} %copy-done), channel_id=1, source_target_pairs={{0,1},{1,0},{2,3},{3,2},{4,5},{5,4},{6,7},{7,6},{8,9},{9,8},{10,11... | collective-permute-start | bytes 1769480 | tf_op jit(solution)/shard_map/ppermute | solution.py:405
  20.1 4.1 %collective-permute-start.4 = (bf16[2304,128]{1,0:T(8,128)(2,1)}, bf16[2304,128]{1,0:T(8,128)(2,1)S(1)}, u32[]{:S(2)}, u32[]{:S(2)}) collective-permute-start(bf16[2304,128]{1,0:T(8,128)(2,1)} %collective-permute-done.2.refs_1_), channel_id=1, source_target_pairs={{0,1},{1,0},{2,3},{3,2},{4,5},{5,4},{6,7},{7,6},{8,9},{9,8},{10,11... | collective-permute-start | bytes 1769480 | tf_op jit(solution)/shard_map/ppermute | solution.py:405
  20.7 3.2 %copy-start.1 = (bf16[512,2048]{1,0:T(8,128)(2,1)S(1)}, bf16[512,2048]{1,0:T(8,128)(2,1)}, u32[]{:S(2)}) copy-start(bf16[512,2048]{1,0:T(8,128)(2,1)} %up_in.1) | copy-start | bytes 6291460
  20.8 3.2 %copy-start.2 = (bf16[2048,512]{1,0:T(8,128)(2,1)S(1)}, bf16[2048,512]{1,0:T(8,128)(2,1)}, u32[]{:S(2)}) copy-start(bf16[2048,512]{1,0:T(8,128)(2,1)} %down_in.1) | copy-start | bytes 6291460
  24.2 2.0 %copy-start.3 = (f32[592,512]{1,0:T(8,128)S(1)}, f32[592,512]{1,0:T(8,128)}, u32[]{:S(2)}) copy-start(f32[592,512]{1,0:T(8,128)} %get-tuple-element.38.resid.resid_b) | copy-start | bytes 3637252
  24.3 2.0 %copy-start.7 = (f32[1,512]{1,0:T(1,128)S(1)}, f32[1,512]{1,0:T(1,128)}, u32[]{:S(2)}) copy-start(f32[1,512]{1,0:T(1,128)} %get-tuple-element.39.gain) | copy-start | bytes 6148
  31.0 4.5 %copy-start.4 = (f32[592,512]{1,0:T(8,128)S(1)}, f32[592,512]{1,0:T(8,128)}, u32[]{:S(2)}) copy-start(f32[592,512]{1,0:T(8,128)} %get-tuple-element.58.resid.resid_a) | copy-start | bytes 3637252
  31.1 10.5 %collective-permute-start.5 = (bf16[320,512]{1,0:T(8,128)(2,1)S(1)}, bf16[320,512]{1,0:T(8,128)(2,1)S(1)}, u32[]{:S(2)}, u32[]{:S(2)}) collective-permute-start(bf16[320,512]{1,0:T(8,128)(2,1)S(1)} %get-tuple-element.57), channel_id=1, source_target_pairs={{1,2},{2,1},{5,6},{6,5},{9,10},{10,9},{13,14},{14,13},{17,18},{18,... | collective-permute-start | bytes 983048 | tf_op jit(solution)/shard_map/ppermute | solution.py:405
  35.2 5.1 %collective-permute-start.6 = (bf16[320,512]{1,0:T(8,128)(2,1)S(1)}, bf16[320,512]{1,0:T(8,128)(2,1)S(1)}, u32[]{:S(2)}, u32[]{:S(2)}) collective-permute-start(bf16[320,512]{1,0:T(8,128)(2,1)S(1)} %get-tuple-element.62), channel_id=1, source_target_pairs={{0,1},{1,0},{2,3},{3,2},{4,5},{5,4},{6,7},{7,6},{8,9},{9,8},{10,11... | collective-permute-start | bytes 983048 | tf_op jit(solution)/shard_map/ppermute | solution.py:405
where the time goes:
time: 46.2 us; the launch traced here: 46.1 us
  Pallas kernels  25.9 us (56%)
  starting transfers between devices  19.4 us (42%)
  between operations  0.48 us (1%)
    ppermute x7, starting transfers between devices, send(): return lax.ppermute(value, AXES, pairs_of(tiles, move))  19.4 us
    pallas_call x2, Pallas kernels, run_half(): call(functools.partial(half_kernel, half), [shape(4, 6, 24, D, dtype=F32)...  9.57 us
    pallas_call x2, Pallas kernels, run_qkv(): call(functools.partial(qkv_kernel, group), [shape(2, 8, 80, 256)] * 3 + [...  5.04 us
    pallas_call x1, Pallas kernels, shards(): call(edge_kernel, shape(4, 2, 6, 24, D), [VMEM] * 25, [pltpu.VMEM((320, 5...  4.3 us
    pallas_call x1, Pallas kernels, shards(): call(norm_kernel, rows + [shape(1, D, dtype=F32)], [HBM] * 6, [pltpu.VMEM...  3.36 us
    pallas_call x1, Pallas kernels, shards(): call(pack_kernel, shape(2304, 128), [HBM] * 4, [pltpu.VMEM((2304, 128), B...  1.95 us
    pallas_call x1, Pallas kernels, shards(): call(first_edge_kernel, shape(2, 144, 256, dtype=F32), [VMEM] * 17, [pltp...  1.28 us
  transfers between devices with their start and end apart: 7, of which 0 were waited for; matrix products, arithmetic and copies ran while one was open for 1% of the time, Pallas kernels for 42%

commit v1 on v0

--- a/solution.py
+++ b/solution.py
@@ -134,7 +134,7 @@
     return total
 
 
-def qkv_kernel(group, norm_a, norm_b, pos_query, pos_key, *refs):
+def qkv_kernel(group, norm_a, norm_b, pos_query, pos_key, after, *refs):
     parts, norms = refs[:2], (norm_a, norm_b)
     query, key, value, wkv, wo, bias_in, bias_edge = refs[2:9]
     wq, left, right = refs[-3:]
@@ -245,8 +245,6 @@
             for k in range(3):
                 at = (pair * 3 + k) * 72 + inner * 36 + col * 6
                 out[level, col, 3 + 6 * k : 9 + 6 * k, :] = inside[at : at + 6, :]
-            out[level, col, :3, :] = jnp.zeros((3, D), F32)
-            out[level, col, 21:, :] = jnp.zeros((3, D), F32)
 
 
 def gather_kernel(count, *refs):
@@ -329,6 +327,10 @@
     wait_all(copies)
 
 
+def tick_kernel(after, out):
+    out[...] = jnp.zeros_like(out)
+
+
 def call(kernel, out_shape, in_specs, scratch=(), limit=16, flops=0, out_specs=None, **extra):
     many = isinstance(out_shape, (list, tuple))
     return pl.pallas_call(
@@ -450,17 +452,19 @@
     places = jnp.asarray(position_tables())
     places = jnp.where(parity == 1, places[1], places[0])
     onehot = (places[:, None] == jnp.arange(256, dtype=jnp.int32)[None, :]).astype(BF)
+    tick = call(tick_kernel, shape(8, 128), [ANY], flops=8 * 10**9, name="tick")(norm_b)
+
     def run_qkv(group, norms, parts):
         return call(
             functools.partial(qkv_kernel, group),
             [shape(2, 8, 80, 256)] * 3
             + [shape(D, 512), shape(256, D)]
             + [shape(2, 2, 288, 144, dtype=F32), shape(2, 2, 2, 160, 160, dtype=F32)],
-            [VMEM] * 6,
+            [VMEM] * 4 + [ANY] + [VMEM] * 2,
             [pltpu.VMEM((D, 256), BF)] + [pltpu.VMEM((128, 256), BF)] * 2,
             flops=2 * 10**9,
             name="qkv_" + str(group),
-        )(*norms, onehot[:304], onehot[304:], *parts)
+        )(*norms, onehot[:304], onehot[304:], tick, *parts)
 
     near = run_qkv(0, (norm_a, norm_b), (own, far))
     up, down = call(

time: 46.2 us -> 46.1 us (level)
  local copies, waits for them, and re-layouts: 0.09 us -> 2.48 us
  Pallas kernels: 25.9 us -> 24.3 us
  starting transfers between devices: 19.4 us -> 18.4 us
    unnamed x20 -> x22, local copies, waits for them, and re-layouts: 0.05 us -> 2.43 us
    pallas_call x2, Pallas kernels: 5.04 us -> 3.81 us  [run_qkv(): call(functools.partial(qkv_kernel, group), [shape(2, 8, 80, 256)] * 3 + [...]
    ppermute x7, starting transfers between devices: 19.4 us -> 18.4 us  [send(): return lax.ppermute(value, AXES, pairs_of(tiles, move))]
  transfers between devices with their start and end apart: 7 -> 7, of which waited for: 0 -> 0; matrix products, arithmetic and copies ran while one was open for 1% -> 1% of each run, Pallas kernels for 42% -> 39%
where the time goes in v1:
time: 46.1 us; the launch traced here: 45.9 us
  Pallas kernels  24.3 us (53%)
  starting transfers between devices  18.4 us (40%)
  local copies, waits for them, and re-layouts  2.48 us (5%)
    ppermute x7, starting transfers between devices, send(): return lax.ppermute(value, AXES, pairs_of(tiles, move))  18.4 us
    pallas_call x2, Pallas kernels, run_half(): call(functools.partial(half_kernel, half), [shape(4, 6, 24, D, dtype=F32)...  9.26 us
    pallas_call x1, Pallas kernels, shards(): call(edge_kernel, shape(4, 2, 6, 24, D), [VMEM] * 25, [pltpu.VMEM((320, 5...  4.3 us
    pallas_call x2, Pallas kernels, run_qkv(): call(functools.partial(qkv_kernel, group), [shape(2, 8, 80, 256)] * 3 + [...  3.81 us
    pallas_call x1, Pallas kernels, shards(): call(norm_kernel, rows + [shape(1, D, dtype=F32)], [HBM] * 6, [pltpu.VMEM...  3.38 us
    unnamed x22, local copies, waits for them, and re-layouts  2.43 us
    pallas_call x1, Pallas kernels, shards(): call(pack_kernel, shape(2304, 128), [HBM] * 4, [pltpu.VMEM((2304, 128), B...  1.95 us
    pallas_call x1, Pallas kernels, shards(): call(first_edge_kernel, shape(2, 144, 256, dtype=F32), [VMEM] * 17, [pltp...  1.28 us
  transfers between devices with their start and end apart: 7, of which 0 were waited for; matrix products, arithmetic and copies ran while one was open for 1% of the time, Pallas kernels for 39%

profile of v1, /device:TPU:1, one launch (start us, length us, event | category | flops | bytes accessed | tf_op | source)
XLA Modules:
  0.0 45.9 jit_solution(8152202126155204996)
XLA Ops:
  0.0 0.0 copy-start.9
  0.0 0.0 copy-start.10
  0.0 2.0 %pack.1.after.refs_0_ = bf16[2304,128]{1,0:T(8,128)(2,1)} custom-call(bf16[1536,128]{1,0:T(8,128)(2,1)} %bitcast.17, bf16[128,512]{1,0:T(8,128)(2,1)} %wo.1, bf16[64,144]{1,0:T(8,128)(2,1)} %bitcast.18, bf16[64,144]{1,0:T(8,128)(2,1)} %bitcast.19), custom_call_target="tpu_custom_call" | custom-call | bytes 2097152 | tf_op jit(solution)/shard_map/pack/pallas_call | solution.py:414
  2.0 3.6 %collective-permute-start.2 = (bf16[2304,128]{1,0:T(8,128)(2,1)}, bf16[2304,128]{1,0:T(8,128)(2,1)S(1)}, u32[]{:S(2)}, u32[]{:S(2)}) collective-permute-start(bf16[2304,128]{1,0:T(8,128)(2,1)} %pack.1.after.refs_0_), channel_id=1, source_target_pairs={{0,2},{1,131},{2,128},{3,1},{4,6},{5,135},{6,132},{7,5},{8,10},{9,... | collective-permute-start | bytes 1769480 | tf_op jit(solution)/shard_map/ppermute | solution.py:407
  5.6 3.4 %norm.1 = (bf16[592,512]{1,0:T(8,128)(2,1)}, bf16[592,512]{1,0:T(8,128)(2,1)}, f32[592,512]{1,0:T(8,128)}, f32[592,512]{1,0:T(8,128)}, f32[1,512]{1,0:T(1,128)}) custom-call(bf16[4,2,6,24,512]{4,3,2,1,0:T(8,128)(2,1)} %bitcast.16, s32[12,24]{1,0:T(8,128)} %bitcast.20, f32[2,512]{1,0:T(2,128)} %embed_in.1, f32[1,512]{1,0:T(1,128)} %bitcast.21, ...), custom_call_target="tpu_custom_call" | custom-call | bytes 2097152 | tf_op jit(solution)/shard_map/norm/pallas_call | solution.py:432
  9.0 1.7 %collective-permute-start = (bf16[592,512]{1,0:T(8,128)(2,1)}, bf16[592,512]{1,0:T(8,128)(2,1)S(1)}, u32[]{:S(2)}, u32[]{:S(2)}) collective-permute-start(bf16[592,512]{1,0:T(8,128)(2,1)} %get-tuple-element.36.after.norm_b.refs_0_), channel_id=1, source_target_pairs={{0,4},{1,5},{2,6},{3,7},{4,0},{5,1},{6,2},{7,3},{8,12},{9,13},{10,... | collective-permute-start | bytes 1818632 | tf_op jit(solution)/shard_map/ppermute | solution.py:407
  10.7 6.9 %collective-permute-start.1 = (bf16[592,512]{1,0:T(8,128)(2,1)}, bf16[592,512]{1,0:T(8,128)(2,1)S(1)}, u32[]{:S(2)}, u32[]{:S(2)}) collective-permute-start(bf16[592,512]{1,0:T(8,128)(2,1)} %get-tuple-element.37.norm_a.refs_2_), channel_id=1, source_target_pairs={{0,252},{1,253},{2,254},{3,255},{4,8},{5,9},{6,10},{7,11},{8,4},{9... | collective-permute-start | bytes 1818632 | tf_op jit(solution)/shard_map/ppermute | solution.py:407
  17.6 0.0 copy-done.9
  17.6 0.0 copy-done.10
  17.7 0.0 copy-start.5
  17.7 1.1 %copy-done.5 = bf16[592,512]{1,0:T(8,128)(2,1)S(1)} copy-done((bf16[592,512]{1,0:T(8,128)(2,1)S(1)}, bf16[592,512]{1,0:T(8,128)(2,1)}, u32[]{:S(2)}) %copy-start.5) | copy-done | bytes 606232
  18.7 0.0 copy-start
  18.8 0.0 copy-start.6
  18.8 0.0 copy-start.7
  18.8 0.0 collective-permute-done.2.refs_1_
  18.8 1.0 %copy-done = bf16[2304,128]{1,0:T(8,128)(2,1)S(1)} copy-done((bf16[2304,128]{1,0:T(8,128)(2,1)S(1)}, bf16[2304,128]{1,0:T(8,128)(2,1)}, u32[]{:S(2)}) %copy-start) | copy-done | bytes 589848
  19.8 2.3 %collective-permute-start.3 = (bf16[2304,128]{1,0:T(8,128)(2,1)S(1)}, bf16[2304,128]{1,0:T(8,128)(2,1)S(1)}, u32[]{:S(2)}, u32[]{:S(2)}) collective-permute-start(bf16[2304,128]{1,0:T(8,128)(2,1)S(1)} %copy-done), channel_id=1, source_target_pairs={{0,1},{1,0},{2,3},{3,2},{4,5},{5,4},{6,7},{7,6},{8,9},{9,8},{10,11... | collective-permute-start | bytes 1769480 | tf_op jit(solution)/shard_map/ppermute | solution.py:407
  22.2 0.0 collective-permute-start.4
  22.2 0.2 fusion
  22.5 0.0 copy-done.6
  22.5 0.0 copy-done.7
  22.5 0.0 copy-start.1
  22.5 0.0 copy-start.2
  22.5 1.9 %qkv_0.1 = (bf16[2,8,80,256]{3,2,1,0:T(8,128)(2,1)S(1)}, bf16[2,8,80,256]{3,2,1,0:T(8,128)(2,1)S(1)}, bf16[2,8,80,256]{3,2,1,0:T(8,128)(2,1)S(1)}, bf16[512,512]...) custom-call(bf16[592,512]{1,0:T(8,128)(2,1)S(1)} %copy-done.7, ...), custom_call_target="tpu_custom_call" | custom-call | flops 2000000000 | bytes 2097152 | tf_op jit(solution)/shard_map/qkv_0/pallas_call | solution.py:458
  24.4 0.0 copy-done.1
  24.4 0.3 copy-done.2
  24.7 0.3 fetch.1
  25.0 0.0 copy-start.3
  25.0 0.0 copy-start.8
  25.0 0.0 collective-permute-done.3.refs_0_
  25.0 0.0 collective-permute-done.4.refs_1_
  25.1 1.9 %qkv_1.1 = (bf16[2,8,80,256]{3,2,1,0:T(8,128)(2,1)S(1)}, bf16[2,8,80,256]{3,2,1,0:T(8,128)(2,1)S(1)}, bf16[2,8,80,256]{3,2,1,0:T(8,128)(2,1)S(1)}, bf16[512,512]...) custom-call(bf16[592,512]{1,0:T(8,128)(2,1)S(1)} %copy-done.7, ...), custom_call_target="tpu_custom_call" | custom-call | flops 2000000000 | bytes 2097152 | tf_op jit(solution)/shard_map/qkv_1/pallas_call | solution.py:458
  27.0 0.0 collective-permute-done.remote.refs_1_
  27.0 0.0 copy-done.3
  27.0 0.0 copy-done.8
  27.0 4.6 %half_b.1 = (f32[4,6,24,512]{3,2,1,0:T(8,128)S(1)}, bf16[2,2,80,256]{3,2,1,0:T(8,128)(2,1)S(1)}, bf16[2,2,80,256]{3,2,1,0:T(8,128)(2,1)S(1)}) custom-call(bf16[592,512]{1,0:T(8,128)(2,1)S(1)} %collective-permute-done.remote.refs_1_, f32[592,512]{1,0:T(8,128)S(1)} %copy-done.3, f32[1,512]{1,0:T(1,128)S(1)} %copy-done.8, ...), custom_call_target="tpu_custom_call" | custom-call | flops 4000000000 | bytes 2097152 | tf_op jit(solution)/shard_map/half_b/pallas_call | solution.py:478
  31.6 0.0 collective-permute-done.1.refs_3_.remote
  31.7 0.0 copy-start.4
  31.7 0.1 gather.1
  31.7 3.4 %collective-permute-start.5 = (bf16[320,512]{1,0:T(8,128)(2,1)S(1)}, bf16[320,512]{1,0:T(8,128)(2,1)S(1)}, u32[]{:S(2)}, u32[]{:S(2)}) collective-permute-start(bf16[320,512]{1,0:T(8,128)(2,1)S(1)} %get-tuple-element.57), channel_id=1, source_target_pairs={{1,2},{2,1},{5,6},{6,5},{9,10},{10,9},{13,14},{14,13},{17,18},{18,... | collective-permute-start | bytes 983048 | tf_op jit(solution)/shard_map/ppermute | solution.py:407
  35.2 0.3 collective-permute-start.6
  35.5 0.0 copy-done.4
  35.5 4.6 %half_a.1 = (f32[4,6,24,512]{3,2,1,0:T(8,128)S(1)}, bf16[2,2,80,256]{3,2,1,0:T(8,128)(2,1)S(1)}, bf16[2,2,80,256]{3,2,1,0:T(8,128)(2,1)S(1)}) custom-call(bf16[592,512]{1,0:T(8,128)(2,1)S(1)} %collective-permute-done.1.refs_3_.remote, f32[592,512]{1,0:T(8,128)S(1)} %copy-done.4, f32[1,512]{1,0:T(1,128)S(1)} %copy-done.8, ...), custom_call_target="tpu_custom_call" | custom-call | flops 4000000000 | bytes 2097152 | tf_op jit(solution)/shard_map/half_a/pallas_call | solution.py:478
  40.1 0.0 collective-permute-done.6.first
  40.1 1.3 %edge_first.1.before = f32[2,144,256]{2,1,0:T(8,128)S(1)} custom-call(bf16[320,512]{1,0:T(8,128)(2,1)S(1)} %collective-permute-done.6.first, bf16[2,2,80,256]{3,2,1,0:T(8,128)(2,1)S(1)} %get-tuple-element.59.key_a, bf16[2,2,80,256]{3,2,1,0:T(8,128)(2,1)S(1)} %get-tuple-element.60.value_a, bf16[2,2,80,256]{3,2,1,0:T(8,128)(2,1)S(1)} %get-tuple-element.56.refs_4_.key_b, ...), custom_call_target="tpu_custom_call" | custom-call | flops 1000000000 | bytes 2097152 | tf_op jit(solution)/shard_map/edge_first/pallas_call | solution.py:504
  41.4 0.0 collective-permute-done.5.second
  41.4 4.3 %edge.1 = bf16[4,2,6,24,512]{4,3,2,1,0:T(8,128)(2,1)} custom-call(bf16[320,512]{1,0:T(8,128)(2,1)S(1)} %collective-permute-done.5.second, bf16[2,2,80,256]{3,2,1,0:T(8,128)(2,1)S(1)} %get-tuple-element.59.key_a, bf16[2,2,80,256]{3,2,1,0:T(8,128)(2,1)S(1)} %get-tuple-element.60.value_a, bf16[2,2,80,256]{3,2,1,0:T(8,128)(2,1)S(1)} %get-tuple-element.56.refs_4_.key_b, ...), custom_call_target="tpu_custom_call" | custom-call | flops 4000000000 | bytes 2097152 | tf_op jit(solution)/shard_map/edge/pallas_call | solution.py:512
  (4 shorter events, 0.1 us)
Async XLA Ops:
  0.0 17.6 %copy-start.9 = (s32[1,1232]{1,0:T(1,128)S(1)}, s32[1,1232]{1,0:T(1,128)}, u32[]{:S(2)}) copy-start(s32[1,1232]{1,0:T(1,128)} %constant.19) | copy-start | bytes 14788
  0.0 17.6 %copy-start.10 = (s32[1,1232]{1,0:T(1,128)S(1)}, s32[1,1232]{1,0:T(1,128)}, u32[]{:S(2)}) copy-start(s32[1,1232]{1,0:T(1,128)} %constant.20) | copy-start | bytes 14788
  2.0 16.8 %collective-permute-start.2 = (bf16[2304,128]{1,0:T(8,128)(2,1)}, bf16[2304,128]{1,0:T(8,128)(2,1)S(1)}, u32[]{:S(2)}, u32[]{:S(2)}) collective-permute-start(bf16[2304,128]{1,0:T(8,128)(2,1)} %pack.1.after.refs_0_), channel_id=1, source_target_pairs={{0,2},{1,131},{2,128},{3,1},{4,6},{5,135},{6,132},{7,5},{8,10},{9,... | collective-permute-start | bytes 1769480 | tf_op jit(solution)/shard_map/ppermute | solution.py:407
  9.0 18.0 %collective-permute-start = (bf16[592,512]{1,0:T(8,128)(2,1)}, bf16[592,512]{1,0:T(8,128)(2,1)S(1)}, u32[]{:S(2)}, u32[]{:S(2)}) collective-permute-start(bf16[592,512]{1,0:T(8,128)(2,1)} %get-tuple-element.36.after.norm_b.refs_0_), channel_id=1, source_target_pairs={{0,4},{1,5},{2,6},{3,7},{4,0},{5,1},{6,2},{7,3},{8,12},{9,13},{10,... | collective-permute-start | bytes 1818632 | tf_op jit(solution)/shard_map/ppermute | solution.py:407
  10.7 20.9 %collective-permute-start.1 = (bf16[592,512]{1,0:T(8,128)(2,1)}, bf16[592,512]{1,0:T(8,128)(2,1)S(1)}, u32[]{:S(2)}, u32[]{:S(2)}) collective-permute-start(bf16[592,512]{1,0:T(8,128)(2,1)} %get-tuple-element.37.norm_a.refs_2_), channel_id=1, source_target_pairs={{0,252},{1,253},{2,254},{3,255},{4,8},{5,9},{6,10},{7,11},{8,4},{9... | collective-permute-start | bytes 1818632 | tf_op jit(solution)/shard_map/ppermute | solution.py:407
  17.7 1.1 %copy-start.5 = (bf16[592,512]{1,0:T(8,128)(2,1)S(1)}, bf16[592,512]{1,0:T(8,128)(2,1)}, u32[]{:S(2)}) copy-start(bf16[592,512]{1,0:T(8,128)(2,1)} %get-tuple-element.36.after.norm_b.refs_0_) | copy-start | bytes 1818628
  18.7 1.1 %copy-start = (bf16[2304,128]{1,0:T(8,128)(2,1)S(1)}, bf16[2304,128]{1,0:T(8,128)(2,1)}, u32[]{:S(2)}) copy-start(bf16[2304,128]{1,0:T(8,128)(2,1)} %pack.1.after.refs_0_) | copy-start | bytes 1769476
  18.8 3.7 %copy-start.6 = (bf16[592,512]{1,0:T(8,128)(2,1)S(1)}, bf16[592,512]{1,0:T(8,128)(2,1)}, u32[]{:S(2)}) copy-start(bf16[592,512]{1,0:T(8,128)(2,1)} %get-tuple-element.36.after.norm_b.refs_0_) | copy-start | bytes 1818628
  18.8 3.7 %copy-start.7 = (bf16[592,512]{1,0:T(8,128)(2,1)S(1)}, bf16[592,512]{1,0:T(8,128)(2,1)}, u32[]{:S(2)}) copy-start(bf16[592,512]{1,0:T(8,128)(2,1)} %get-tuple-element.37.norm_a.refs_2_) | copy-start | bytes 1818628
  19.8 5.2 %collective-permute-start.3 = (bf16[2304,128]{1,0:T(8,128)(2,1)S(1)}, bf16[2304,128]{1,0:T(8,128)(2,1)S(1)}, u32[]{:S(2)}, u32[]{:S(2)}) collective-permute-start(bf16[2304,128]{1,0:T(8,128)(2,1)S(1)} %copy-done), channel_id=1, source_target_pairs={{0,1},{1,0},{2,3},{3,2},{4,5},{5,4},{6,7},{7,6},{8,9},{9,8},{10,11... | collective-permute-start | bytes 1769480 | tf_op jit(solution)/shard_map/ppermute | solution.py:407
  22.2 2.9 %collective-permute-start.4 = (bf16[2304,128]{1,0:T(8,128)(2,1)S(1)}, bf16[2304,128]{1,0:T(8,128)(2,1)S(1)}, u32[]{:S(2)}, u32[]{:S(2)}) collective-permute-start(bf16[2304,128]{1,0:T(8,128)(2,1)S(1)} %collective-permute-done.2.refs_1_), channel_id=1, source_target_pairs={{0,1},{1,0},{2,3},{3,2},{4,5},{5,4},{6,7},{7,6},{8,9},{9,8},{10,11... | collective-permute-start | bytes 1769480 | tf_op jit(solution)/shard_map/ppermute | solution.py:407
  22.5 1.9 %copy-start.1 = (bf16[512,2048]{1,0:T(8,128)(2,1)S(1)}, bf16[512,2048]{1,0:T(8,128)(2,1)}, u32[]{:S(2)}) copy-start(bf16[512,2048]{1,0:T(8,128)(2,1)} %up_in.1) | copy-start | bytes 6291460
  22.5 2.2 %copy-start.2 = (bf16[2048,512]{1,0:T(8,128)(2,1)S(1)}, bf16[2048,512]{1,0:T(8,128)(2,1)}, u32[]{:S(2)}) copy-start(bf16[2048,512]{1,0:T(8,128)(2,1)} %down_in.1) | copy-start | bytes 6291460
  25.0 2.0 %copy-start.3 = (f32[592,512]{1,0:T(8,128)S(1)}, f32[592,512]{1,0:T(8,128)}, u32[]{:S(2)}) copy-start(f32[592,512]{1,0:T(8,128)} %get-tuple-element.38.resid.resid_b) | copy-start | bytes 3637252
  25.0 2.0 %copy-start.8 = (f32[1,512]{1,0:T(1,128)S(1)}, f32[1,512]{1,0:T(1,128)}, u32[]{:S(2)}) copy-start(f32[1,512]{1,0:T(1,128)} %get-tuple-element.39.gain) | copy-start | bytes 6148
  31.7 3.8 %copy-start.4 = (f32[592,512]{1,0:T(8,128)S(1)}, f32[592,512]{1,0:T(8,128)}, u32[]{:S(2)}) copy-start(f32[592,512]{1,0:T(8,128)} %get-tuple-element.58.resid.resid_a) | copy-start | bytes 3637252
  31.7 9.7 %collective-permute-start.5 = (bf16[320,512]{1,0:T(8,128)(2,1)S(1)}, bf16[320,512]{1,0:T(8,128)(2,1)S(1)}, u32[]{:S(2)}, u32[]{:S(2)}) collective-permute-start(bf16[320,512]{1,0:T(8,128)(2,1)S(1)} %get-tuple-element.57), channel_id=1, source_target_pairs={{1,2},{2,1},{5,6},{6,5},{9,10},{10,9},{13,14},{14,13},{17,18},{18,... | collective-permute-start | bytes 983048 | tf_op jit(solution)/shard_map/ppermute | solution.py:407
  35.2 5.0 %collective-permute-start.6 = (bf16[320,512]{1,0:T(8,128)(2,1)S(1)}, bf16[320,512]{1,0:T(8,128)(2,1)S(1)}, u32[]{:S(2)}, u32[]{:S(2)}) collective-permute-start(bf16[320,512]{1,0:T(8,128)(2,1)S(1)} %get-tuple-element.62), channel_id=1, source_target_pairs={{0,1},{1,0},{2,3},{3,2},{4,5},{5,4},{6,7},{7,6},{8,9},{9,8},{10,11... | collective-permute-start | bytes 983048 | tf_op jit(solution)/shard_map/ppermute | solution.py:407
